TPU v7x, 32 devices: a whole 2x2x4 slice. The times are simulated.
32 devices in a mesh: space: 8 (over z, x), member: 4 (over y, core).
Axes of the slice: x: 2, y: 2, z: 4, core: 2. Of those that a mesh axis runs over, the one named last changes fastest.
Arguments:
- fields: float32 [8, 16, 128, 256], P('member', 'space'), may hold values from -6 to 6
- velocity: float32 [16, 128, 256], P('space'), may hold values from 0.2 to 0.6
- building: int32 [16, 128, 256], P('space'), may hold values 0 or 1
- inflow_table: float32 [32, 128, 256], replicated, may hold values from -6 to 6
- inflow_index: int32 [8], P('member'), may hold values from 0 to 31
Outputs:
- fields_now: float32 [8, 16, 128, 256], P('member', 'space')
- r_factor: float32 [8, 8], replicated
All inputs are finite; a program needn't handle non-finite values. No bound on the sum of `building` on one device may be relied on, other than what follows from the above.
Results may differ from a plain program's by a relative error of at most 0.0003.
Values may be sent and summed in bfloat16 or wider, within the bound.
A program may use at most 64 MiB of HBM per device.

v0:
```python
import jax
import jax.numpy as jnp
from jax import lax
from jax.sharding import PartitionSpec as P

STEPS = 2
kappa_rate = 0.05
shrink_weight = 0.1
contract_dims = (((1,), (1,)), ((), ()))


def extended_2(block, sides, width):
    for axis, dim in sides:
        count = lax.axis_size(axis)
        forward = [(i, i + 1) for i in range(count - 1)]
        backward = [(target, source) for source, target in forward]
        low = lax.ppermute(
            lax.slice_in_dim(block, block.shape[dim] - width, None, axis=dim), axis, forward
        )
        high = lax.ppermute(lax.slice_in_dim(block, 0, width, axis=dim), axis, backward)
        block = jnp.concatenate([low, block, high], axis=dim)
    return block


def from_behind(block, axis, distance):
    devices = range(lax.axis_size(axis))
    route = [((i - distance) % len(devices), i) for i in devices]
    return lax.ppermute(block, axis, route)


def advance(extended, fluid_cells, courant):
    upwind = extended[:, :-2]
    centre = extended[:, 1:-1]
    downwind = extended[:, 2:]
    in_plane = (
        jnp.roll(centre, 1, 2)
        + jnp.roll(centre, -1, 2)
        + jnp.roll(centre, 1, 3)
        + jnp.roll(centre, -1, 3)
    )
    return fluid_cells * (
        centre
        + courant * (upwind - centre)
        + kappa_rate * (upwind + downwind + in_plane - 6.0 * centre)
    )


def local(fields, velocity, building, inflow_table, inflow_index):
    mem_dev = fields.shape[0]
    slab_depth = fields.shape[1]
    plane_rows = fields.shape[2]
    plane_cols = fields.shape[3]
    patterns = inflow_table.shape[0]
    fluid_cells = (1 - building).astype(jnp.float32)
    pattern_pick = (inflow_index[:, None] == jnp.arange(patterns, dtype=jnp.int32)[None, :]).astype(
        jnp.float32
    )
    inflow_plane = jnp.dot(
        pattern_pick,
        inflow_table.reshape(patterns, plane_rows * plane_cols),
        precision=lax.Precision.HIGHEST,
        preferred_element_type=jnp.float32,
    ).reshape(mem_dev, plane_rows, plane_cols)
    at_inflow = lax.axis_index("space") == 0
    fields_now = fields
    for sweep_index in range(STEPS):
        extended = extended_2(fields_now, (("space", 1),), 1)
        extended = extended.at[:, 0].set(jnp.where(at_inflow, inflow_plane, extended[:, 0]))
        fields_now = advance(extended, fluid_cells, velocity)
    groups = lax.axis_size("member")
    all_members = mem_dev * groups
    member_sum = jnp.sum(fields_now, 0)
    ensemble_mean = (
        lax.psum(member_sum.astype(jnp.bfloat16), "member").astype(jnp.float32) / all_members
    )
    anomaly = (
        (fields_now - ensemble_mean)
        .astype(jnp.bfloat16)
        .reshape(mem_dev, slab_depth * plane_rows * plane_cols)
    )
    my_group = lax.axis_index("member")
    cells_all = slab_depth * lax.axis_size("space") * plane_rows * plane_cols
    empty_rows = jnp.zeros((mem_dev, all_members), jnp.float32)

    def place(gram_tile, panel_piece, first_row):
        gram_block = lax.dot_general(
            anomaly, panel_piece, contract_dims, preferred_element_type=jnp.float32
        )
        return lax.dynamic_update_slice(
            gram_tile, gram_block, (jnp.int32(0), jnp.asarray(first_row))
        )

    gram_tile = place(empty_rows, anomaly, my_group * mem_dev)

    def turn(sweep_index, loop_state):
        tile_now, panel_held = loop_state
        panel_held = from_behind(panel_held, "member", 1)
        source = (my_group - sweep_index) % groups
        return (place(tile_now, panel_held, source * mem_dev), panel_held)

    gram_tile, panel_held = lax.fori_loop(1, groups, turn, (gram_tile, anomaly))
    gram_tile = gram_tile / cells_all
    summed = lax.psum(gram_tile, "space")
    gram_full = lax.all_gather(summed, "member", axis=0, tiled=True)
    r_factor = jnp.linalg.cholesky(
        gram_full + shrink_weight * jnp.eye(all_members, dtype=jnp.float32)
    ).T
    return (fields_now, r_factor)


def solution(mesh):
    placed = (
        P("member", "space", None, None),
        P("space", None, None),
        P("space", None, None),
        P(),
        P("member"),
    )
    return jax.shard_map(
        local,
        mesh=mesh,
        in_specs=placed,
        out_specs=(P("member", "space", None, None), P()),
        check_vma=False,
    )
```

profile of v0, /device:TPU:0, one launch (start us, length us, event | category | flops | bytes accessed | tf_op | source)
XLA Modules:
  0.0 151.2 jit_solution(6526579312249673913)
XLA Ops:
  7.2 1.4 copy.24
  8.9 4.9 %collective-permute-start.1 = (f32[2,1,128,256]{3,0,2,1:T(2,128)S(1)}, f32[2,1,128,256]{3,0,2,1:T(2,128)S(1)}, u32[]{:S(2)}, u32[]{:S(2)}) collective-permute-start(f32[2,1,128,256]{3,0,2,1:T(2,128)S(1)} %get-tuple-element.196), channel_id=1, source_target_pairs={{0,4},{4,8},{8,12},{12,16},{16,20},{20,24},{24,28},{1,5},{5,9},{9,... | collective-permute-start | bytes 786440 | tf_op jit(solution)/shard_map/ppermute | solution.py:17
  13.7 1.3 collective-permute-start.2
  15.0 1.0 subtract_convert_fusion.1
  16.0 8.9 %collective-permute-done.1 = f32[2,1,128,256]{3,0,2,1:T(2,128)S(1)} collective-permute-done((f32[2,1,128,256]{3,0,2,1:T(2,128)S(1)}, f32[2,1,128,256]{3,0,2,1:T(2,128)S(1)}, u32[]{:S(2)}, u32[]{:S(2)}) %collective-permute-start.1) | collective-permute-done | bytes 262176 | tf_op jit(solution)/shard_map/ppermute | solution.py:17
  25.4 6.0 %bitcast_dynamic-update-slice_fusion.1 = (f32[2,4,128,256]{3,0,2,1:T(2,128)S(1)}, f32[2,128,256]{2,0,1:T(2,128)S(1)}) fusion(f32[2,4,128,256]{3,0,2,1:T(2,128)S(1)} %pad_maximum_fusion, f32[2,1,128,256]{3,0,2,1:T(2,128)S(1)} %collective-permute-done.1, pred[]{:T(512)S(6)} %eq.25, s32[2]{0:T(128)S(1)} %copy-done.1, f32[4,8,128,256]{3,2,1,0:T(8,128)} %bitcast.51), kind=kOutput, calls=%fused_computation.27 | convolution fusion | flops 25231424 | bytes 4981249 | tf_op jit(solution)/shard_map/dot_general | solution.py:58
  32.7 1.9 %fusion.15 = f32[2,2,128,256]{3,0,2,1:T(2,128)S(1)} fusion(f32[2,2,128,1]{3,0,2,1:T(2,128)S(1)} %get-tuple-element.191, f32[2,2,128,255]{3,0,2,1:T(2,128)S(1)} %get-tuple-element.193, f32[2,2,128,255]{3,0,2,1:T(2,128)S(1)} %get-tuple-element.192, f32[2,2,128,1]{3,0,2,1:T(2,128)S(1)} %get-tuple-element.190, f32[2,2,1,256]{3,0,2,1:T(2,128)S(1)} %get-tuple-element.187, ...), kind=kLoop, calls=%fused_computation.23 | loop fusion | flops 2228224 | bytes 4718592 | tf_op jit(solution)/shard_map/mul | solution.py:41
  34.8 4.4 %collective-permute-start.3 = (f32[2,1,128,256]{3,0,2,1:T(2,128)S(1)}, f32[2,1,128,256]{3,0,2,1:T(2,128)S(1)}, u32[]{:S(2)}, u32[]{:S(2)}) collective-permute-start(f32[2,1,128,256]{3,0,2,1:T(2,128)S(1)} %get-tuple-element.194), channel_id=1, source_target_pairs={{0,4},{4,8},{8,12},{12,16},{16,20},{20,24},{24,28},{1,5},{5,9},{9,... | collective-permute-start | bytes 786440 | tf_op jit(solution)/shard_map/ppermute | solution.py:17
  39.3 1.5 collective-permute-start.4
  40.7 3.2 %collective-permute-done.3 = f32[2,1,128,256]{3,0,2,1:T(2,128)S(1)} collective-permute-done((f32[2,1,128,256]{3,0,2,1:T(2,128)S(1)}, f32[2,1,128,256]{3,0,2,1:T(2,128)S(1)}, u32[]{:S(2)}, u32[]{:S(2)}) %collective-permute-start.3) | collective-permute-done | bytes 262176 | tf_op jit(solution)/shard_map/ppermute | solution.py:17
  43.9 5.9 %collective-permute-done.4 = f32[2,1,128,256]{3,0,2,1:T(2,128)S(1)} collective-permute-done((f32[2,1,128,256]{3,0,2,1:T(2,128)S(1)}, f32[2,1,128,256]{3,0,2,1:T(2,128)S(1)}, u32[]{:S(2)}, u32[]{:S(2)}) %collective-permute-start.4) | collective-permute-done | bytes 262176 | tf_op jit(solution)/shard_map/ppermute | solution.py:20
  51.8 3.2 %fusion.22 = (bf16[2,128,256]{2,1,0:T(8,128)(2,1)}, f32[2,2,128,256]{3,0,2,1:T(2,128)S(1)}) fusion(f32[2,2,128,1]{3,0,2,1:T(2,128)S(1)} %get-tuple-element.183, f32[2,2,128,255]{3,0,2,1:T(2,128)S(1)} %get-tuple-element.185, f32[2,2,128,255]{3,0,2,1:T(2,128)S(1)} %get-tuple-element.184, f32[2,2,128,1]{3,0,2,1:T(2,128)S(1)} %get-tuple-element.182, ...), kind=kLoop, calls=%fused_computation.44 | loop fusion | flops 2293760 | bytes 4849664 | tf_op jit(solution)/shard_map/reduce_sum | solution.py:72
  55.0 35.5 %all-reduce.2.cloned.1.call-done = bf16[2,128,256]{2,1,0:T(8,128)(2,1)} async-done(((bf16[2,128,256]{2,1,0:T(8,128)(2,1)}), bf16[2,128,256]{2,1,0:T(8,128)(2,1)}) %all-reduce.2.cloned.1.call-update) | async-done | bytes 131088 | tf_op jit(solution)/shard_map/psum | solution.py:74
  90.5 0.9 convert_multiply_fusion
  91.7 0.9 convolution_bitcast_fusion
  92.9 21.1 %while.19 = (s32[]{:T(128)}, f32[2,8]{1,0:T(2,128)S(1)}, bf16[2,65536]{1,0:T(2,128)(2,1)S(1)}, bf16[2,65536]{1,0:T(2,128)(2,1)S(1)}, s32[]{:T(128)}, /*index=5*/...) while((s32[]{:T(128)}, f32[2,8]{1,0:T(2,128)S(1)}, ...), condition=%wide.region_3.4_spmd, body=%wide.region_2.3_spmd.sunk | while | flops 524306 | bytes 2097520 | solution.py:101
  93.0 5.8 %collective-permute-done = bf16[2,65536]{1,0:T(2,128)(2,1)S(1)} collective-permute-done((bf16[2,65536]{1,0:T(2,128)(2,1)S(1)}, bf16[2,65536]{1,0:T(2,128)(2,1)S(1)}, u32[]{:S(2)}, u32[]{:S(2)}) %collective-permute-start) | collective-permute-done | bytes 262176 | tf_op jit(solution)/shard_map/while/body/eval_jaxpr/ppermute | solution.py:28
  98.8 0.8 fusion.44
  100.0 5.8 %collective-permute-done = bf16[2,65536]{1,0:T(2,128)(2,1)S(1)} collective-permute-done((bf16[2,65536]{1,0:T(2,128)(2,1)S(1)}, bf16[2,65536]{1,0:T(2,128)(2,1)S(1)}, u32[]{:S(2)}, u32[]{:S(2)}) %collective-permute-start) | collective-permute-done | bytes 262176 | tf_op jit(solution)/shard_map/while/body/eval_jaxpr/ppermute | solution.py:28
  107.1 5.8 %collective-permute-done = bf16[2,65536]{1,0:T(2,128)(2,1)S(1)} collective-permute-done((bf16[2,65536]{1,0:T(2,128)(2,1)S(1)}, bf16[2,65536]{1,0:T(2,128)(2,1)S(1)}, u32[]{:S(2)}, u32[]{:S(2)}) %collective-permute-start) | collective-permute-done | bytes 262176 | tf_op jit(solution)/shard_map/while/body/eval_jaxpr/ppermute | solution.py:28
  114.0 0.8 copy.32
  114.9 21.3 %psum.15 = f32[2,8]{1,0:T(2,128)S(1)} all-reduce(f32[2,8]{1,0:T(2,128)S(1)} %broadcast_multiply_fusion), channel_id=1, replica_groups=mesh['space'=8,'member'=4] {'space'}, use_global_device_ids=true, to_apply=%region_4.5 | all-reduce | flops 16 | bytes 128 | tf_op jit(solution)/shard_map/psum | solution.py:103
  136.2 5.1 %all-gather = f32[4,2,8]{2,1,0:T(2,128)S(1)} all-gather(f32[1,2,8]{2,1,0:T(2,128)S(1)} %bitcast.55), channel_id=1, replica_groups=mesh['space'=8,'member'=4] {'member'}, dimensions={0}, use_global_device_ids=true | all-gather | bytes 320 | tf_op jit(solution)/shard_map/all_gather | solution.py:104
  143.1 1.3 select_bitcast_fusion
  (44 shorter events, 9.5 us)
Async XLA Ops:
  7.2 18.2 %copy-start.1 = (s32[2]{0:T(128)S(1)}, s32[2]{0:T(128)}, u32[]{:S(2)}) copy-start(s32[2]{0:T(128)} %param.15) | copy-start | bytes 28
  7.2 83.3 %all-reduce.2.cloned.1.call-start = ((), (), s32[]{:S(2)}) async-start(), calls=%async_computation | async-start | bytes 262144 | tf_op jit(solution)/shard_map/psum | solution.py:74
  8.9 16.0 %collective-permute-start.1 = (f32[2,1,128,256]{3,0,2,1:T(2,128)S(1)}, f32[2,1,128,256]{3,0,2,1:T(2,128)S(1)}, u32[]{:S(2)}, u32[]{:S(2)}) collective-permute-start(f32[2,1,128,256]{3,0,2,1:T(2,128)S(1)} %get-tuple-element.196), channel_id=1, source_target_pairs={{0,4},{4,8},{8,12},{12,16},{16,20},{20,24},{24,28},{1,5},{5,9},{9,... | collective-permute-start | bytes 786440 | tf_op jit(solution)/shard_map/ppermute | solution.py:17
  13.7 11.2 %collective-permute-start.2 = (f32[2,1,128,256]{3,0,2,1:T(2,128)S(1)}, f32[2,1,128,256]{3,0,2,1:T(2,128)S(1)}, u32[]{:S(2)}, u32[]{:S(2)}) collective-permute-start(f32[2,1,128,256]{3,0,2,1:T(2,128)S(1)} %get-tuple-element.197), channel_id=1, source_target_pairs={{4,0},{8,4},{12,8},{16,12},{20,16},{24,20},{28,24},{5,1},{9,5},{13... | collective-permute-start | bytes 786440 | tf_op jit(solution)/shard_map/ppermute | solution.py:20
  25.4 7.3 %copy-start = (f32[2,128,256]{2,1,0:T(8,128)S(1)}, f32[2,128,256]{2,1,0:T(8,128)}, u32[]{:S(2)}) copy-start(f32[2,128,256]{2,1,0:T(8,128)} %param.12) | copy-start | bytes 786436
  34.8 9.1 %collective-permute-start.3 = (f32[2,1,128,256]{3,0,2,1:T(2,128)S(1)}, f32[2,1,128,256]{3,0,2,1:T(2,128)S(1)}, u32[]{:S(2)}, u32[]{:S(2)}) collective-permute-start(f32[2,1,128,256]{3,0,2,1:T(2,128)S(1)} %get-tuple-element.194), channel_id=1, source_target_pairs={{0,4},{4,8},{8,12},{12,16},{16,20},{20,24},{24,28},{1,5},{5,9},{9,... | collective-permute-start | bytes 786440 | tf_op jit(solution)/shard_map/ppermute | solution.py:17
  39.3 10.5 %collective-permute-start.4 = (f32[2,1,128,256]{3,0,2,1:T(2,128)S(1)}, f32[2,1,128,256]{3,0,2,1:T(2,128)S(1)}, u32[]{:S(2)}, u32[]{:S(2)}) collective-permute-start(f32[2,1,128,256]{3,0,2,1:T(2,128)S(1)} %get-tuple-element.195), channel_id=1, source_target_pairs={{4,0},{8,4},{12,8},{16,12},{20,16},{24,20},{28,24},{5,1},{9,5},{13... | collective-permute-start | bytes 786440 | tf_op jit(solution)/shard_map/ppermute | solution.py:20
  92.9 5.8 %collective-permute-start = (bf16[2,65536]{1,0:T(2,128)(2,1)S(1)}, bf16[2,65536]{1,0:T(2,128)(2,1)S(1)}, u32[]{:S(2)}, u32[]{:S(2)}) collective-permute-start(bf16[2,65536]{1,0:T(2,128)(2,1)S(1)} %get-tuple-element.244), channel_id=1, source_target_pairs={{3,0},{0,1},{1,2},{2,3},{7,4},{4,5},{5,6},{6,7},{11,8},{8,9},{9,10... | collective-permute-start | bytes 786440 | tf_op jit(solution)/shard_map/while/body/eval_jaxpr/ppermute | solution.py:28
  99.9 5.8 %collective-permute-start = (bf16[2,65536]{1,0:T(2,128)(2,1)S(1)}, bf16[2,65536]{1,0:T(2,128)(2,1)S(1)}, u32[]{:S(2)}, u32[]{:S(2)}) collective-permute-start(bf16[2,65536]{1,0:T(2,128)(2,1)S(1)} %get-tuple-element.244), channel_id=1, source_target_pairs={{3,0},{0,1},{1,2},{2,3},{7,4},{4,5},{5,6},{6,7},{11,8},{8,9},{9,10... | collective-permute-start | bytes 786440 | tf_op jit(solution)/shard_map/while/body/eval_jaxpr/ppermute | solution.py:28
  107.0 5.8 %collective-permute-start = (bf16[2,65536]{1,0:T(2,128)(2,1)S(1)}, bf16[2,65536]{1,0:T(2,128)(2,1)S(1)}, u32[]{:S(2)}, u32[]{:S(2)}) collective-permute-start(bf16[2,65536]{1,0:T(2,128)(2,1)S(1)} %get-tuple-element.244), channel_id=1, source_target_pairs={{3,0},{0,1},{1,2},{2,3},{7,4},{4,5},{5,6},{6,7},{11,8},{8,9},{9,10... | collective-permute-start | bytes 786440 | tf_op jit(solution)/shard_map/while/body/eval_jaxpr/ppermute | solution.py:28
Sparse Core Ops, SparseCore 0:
  55.1 35.3 all-reduce.1
where the time goes:
time: 151 us
  waiting for transfers between devices  70.7 us (47%)
  blocking collectives  26.4 us (17%)
  between operations  14.3 us (9%)
  starting transfers between devices  12.2 us (8%)
  other arithmetic  11.2 us (7%)
  matrix products  9.16 us (6%)
  local copies, waits for them, and re-layouts  7.04 us (5%)
    psum x1, waiting for transfers between devices, local(): lax.psum(member_sum.astype(jnp.bfloat16), 'member').astype(jnp.float32)  35.5 us
    psum x1, blocking collectives, local(): summed = lax.psum(gram_tile, 'space')  21.3 us
    ppermute x3, waiting for transfers between devices, from_behind(): return lax.ppermute(block, axis, route)  17.3 us
    ppermute x2, waiting for transfers between devices, extended_2(): lax.ppermute(lax.slice_in_dim(block, block.shape[dim] - width, None, axis...  12 us
    ppermute x2, starting transfers between devices, extended_2(): lax.ppermute(lax.slice_in_dim(block, block.shape[dim] - width, None, axis...  9.26 us
    dot_general x1, matrix products, local(): jnp.dot(pattern_pick, inflow_table.reshape(patterns, plane_rows * plane_c...  5.97 us
    ppermute x2, waiting for transfers between devices, extended_2(): lax.ppermute(lax.slice_in_dim(block, 0, width, axis=dim), axis, backward)  5.88 us
    all_gather x1, blocking collectives, local(): gram_full = lax.all_gather(summed, 'member', axis=0, tiled=True)  5.06 us
  transfers between devices with their start and end apart: 8, of which 7 were waited for; matrix products, arithmetic and copies ran while one was open for 1% of the time, Pallas kernels for 0%

commit v1 on v0

--- a/solution.py
+++ b/solution.py
@@ -71,7 +71,10 @@
     all_members = mem_dev * groups
     member_sum = jnp.sum(fields_now, 0)
     ensemble_mean = (
-        lax.psum(member_sum.astype(jnp.bfloat16), "member").astype(jnp.float32) / all_members
+        jnp.sum(lax.all_gather(member_sum.astype(jnp.bfloat16), "member"), axis=0).astype(
+            jnp.float32
+        )
+        / all_members
     )
     anomaly = (
         (fields_now - ensemble_mean)

time: 151 us -> 110 us (0.73)
  waiting for transfers between devices: 70.7 us -> 35 us
  between operations: 14.3 us -> 0.89 us
  blocking collectives: 26.4 us -> 35.7 us
  other arithmetic: 11.2 us -> 9.55 us
    psum x1 -> x0, waiting for transfers between devices: 35.5 us -> none  [local(): lax.psum(member_sum.astype(jnp.bfloat16), 'member').astype(jnp.float32)]
    all_gather x0 -> x1, blocking collectives: none -> 7.38 us  [local(): lax.all_gather(member_sum.astype(jnp.bfloat16), 'member')]
    psum x1, blocking collectives: 21.3 us -> 23.3 us  [local(): summed = lax.psum(gram_tile, 'space')]
  transfers between devices with their start and end apart: 8 -> 7, of which waited for: 7 -> 6; matrix products, arithmetic and copies ran while one was open for 1% -> 1% of each run, Pallas kernels for 0% -> 0%
where the time goes in v1:
time: 110 us
  blocking collectives  35.7 us (32%)
  waiting for transfers between devices  35 us (32%)
  starting transfers between devices  12.4 us (11%)
  other arithmetic  9.55 us (9%)
  matrix products  9.16 us (8%)
  local copies, waits for them, and re-layouts  7.05 us (6%)
    psum x1, blocking collectives, local(): summed = lax.psum(gram_tile, 'space')  23.3 us
    ppermute x3, waiting for transfers between devices, from_behind(): return lax.ppermute(block, axis, route)  16.9 us
    ppermute x2, waiting for transfers between devices, extended_2(): lax.ppermute(lax.slice_in_dim(block, block.shape[dim] - width, None, axis...  12.2 us
    ppermute x2, starting transfers between devices, extended_2(): lax.ppermute(lax.slice_in_dim(block, block.shape[dim] - width, None, axis...  9.26 us
    all_gather x1, blocking collectives, local(): lax.all_gather(member_sum.astype(jnp.bfloat16), 'member')  7.38 us
    dot_general x1, matrix products, local(): jnp.dot(pattern_pick, inflow_table.reshape(patterns, plane_rows * plane_c...  5.97 us
    ppermute x2, waiting for transfers between devices, extended_2(): lax.ppermute(lax.slice_in_dim(block, 0, width, axis=dim), axis, backward)  5.88 us
    all_gather x1, blocking collectives, local(): gram_full = lax.all_gather(summed, 'member', axis=0, tiled=True)  5.06 us
  transfers between devices with their start and end apart: 7, of which 6 were waited for; matrix products, arithmetic and copies ran while one was open for 1% of the time, Pallas kernels for 0%

profile of v1, /device:TPU:0, one launch (start us, length us, event | category | flops | bytes accessed | tf_op | source)
XLA Modules:
  0.0 109.9 jit_solution(15903435040732537734)
XLA Ops:
  0.6 1.5 %copy.24 = f32[2,2,128,256]{3,0,2,1:T(2,128)S(1)} copy(f32[2,2,128,256]{3,2,1,0:T(8,128)} %param.11) | data formatting | bytes 1048576 | tf_op args[0]
  2.3 4.9 %collective-permute-start.1 = (f32[2,1,128,256]{3,0,2,1:T(2,128)S(1)}, f32[2,1,128,256]{3,0,2,1:T(2,128)S(1)}, u32[]{:S(2)}, u32[]{:S(2)}) collective-permute-start(f32[2,1,128,256]{3,0,2,1:T(2,128)S(1)} %get-tuple-element.196), channel_id=1, source_target_pairs={{0,4},{4,8},{8,12},{12,16},{16,20},{20,24},{24,28},{1,5},{5,9},{9,... | collective-permute-start | bytes 786440 | tf_op jit(solution)/shard_map/ppermute | solution.py:17
  7.2 1.3 %collective-permute-start.2 = (f32[2,1,128,256]{3,0,2,1:T(2,128)S(1)}, f32[2,1,128,256]{3,0,2,1:T(2,128)S(1)}, u32[]{:S(2)}, u32[]{:S(2)}) collective-permute-start(f32[2,1,128,256]{3,0,2,1:T(2,128)S(1)} %get-tuple-element.197), channel_id=1, source_target_pairs={{4,0},{8,4},{12,8},{16,12},{20,16},{24,20},{28,24},{5,1},{9,5},{13... | collective-permute-start | bytes 786440 | tf_op jit(solution)/shard_map/ppermute | solution.py:20
  8.5 1.0 subtract_convert_fusion.1
  9.4 8.9 %collective-permute-done.1 = f32[2,1,128,256]{3,0,2,1:T(2,128)S(1)} collective-permute-done((f32[2,1,128,256]{3,0,2,1:T(2,128)S(1)}, f32[2,1,128,256]{3,0,2,1:T(2,128)S(1)}, u32[]{:S(2)}, u32[]{:S(2)}) %collective-permute-start.1) | collective-permute-done | bytes 262176 | tf_op jit(solution)/shard_map/ppermute | solution.py:17
  18.8 6.0 %bitcast_dynamic-update-slice_fusion.1 = (f32[2,4,128,256]{3,0,2,1:T(2,128)S(1)}, f32[2,128,256]{2,0,1:T(2,128)S(1)}) fusion(f32[2,4,128,256]{3,0,2,1:T(2,128)S(1)} %pad_maximum_fusion, f32[2,1,128,256]{3,0,2,1:T(2,128)S(1)} %collective-permute-done.1, pred[]{:T(512)S(6)} %eq.25, s32[2]{0:T(128)S(1)} %copy-done.1, f32[4,8,128,256]{3,2,1,0:T(8,128)} %bitcast.52), kind=kOutput, calls=%fused_computation.27 | convolution fusion | flops 25231424 | bytes 4981249 | tf_op jit(solution)/shard_map/dot_general | solution.py:58
  26.1 1.9 %fusion.15 = f32[2,2,128,256]{3,0,2,1:T(2,128)S(1)} fusion(f32[2,2,128,1]{3,0,2,1:T(2,128)S(1)} %get-tuple-element.191, f32[2,2,128,255]{3,0,2,1:T(2,128)S(1)} %get-tuple-element.193, f32[2,2,128,255]{3,0,2,1:T(2,128)S(1)} %get-tuple-element.192, f32[2,2,128,1]{3,0,2,1:T(2,128)S(1)} %get-tuple-element.190, f32[2,2,1,256]{3,0,2,1:T(2,128)S(1)} %get-tuple-element.187, ...), kind=kLoop, calls=%fused_computation.23 | loop fusion | flops 2228224 | bytes 4718592 | tf_op jit(solution)/shard_map/mul | solution.py:41
  28.3 4.4 %collective-permute-start.3 = (f32[2,1,128,256]{3,0,2,1:T(2,128)S(1)}, f32[2,1,128,256]{3,0,2,1:T(2,128)S(1)}, u32[]{:S(2)}, u32[]{:S(2)}) collective-permute-start(f32[2,1,128,256]{3,0,2,1:T(2,128)S(1)} %get-tuple-element.194), channel_id=1, source_target_pairs={{0,4},{4,8},{8,12},{12,16},{16,20},{20,24},{24,28},{1,5},{5,9},{9,... | collective-permute-start | bytes 786440 | tf_op jit(solution)/shard_map/ppermute | solution.py:17
  32.7 1.3 %collective-permute-start.4 = (f32[2,1,128,256]{3,0,2,1:T(2,128)S(1)}, f32[2,1,128,256]{3,0,2,1:T(2,128)S(1)}, u32[]{:S(2)}, u32[]{:S(2)}) collective-permute-start(f32[2,1,128,256]{3,0,2,1:T(2,128)S(1)} %get-tuple-element.195), channel_id=1, source_target_pairs={{4,0},{8,4},{12,8},{16,12},{20,16},{24,20},{28,24},{5,1},{9,5},{13... | collective-permute-start | bytes 786440 | tf_op jit(solution)/shard_map/ppermute | solution.py:20
  34.0 3.4 %collective-permute-done.3 = f32[2,1,128,256]{3,0,2,1:T(2,128)S(1)} collective-permute-done((f32[2,1,128,256]{3,0,2,1:T(2,128)S(1)}, f32[2,1,128,256]{3,0,2,1:T(2,128)S(1)}, u32[]{:S(2)}, u32[]{:S(2)}) %collective-permute-start.3) | collective-permute-done | bytes 262176 | tf_op jit(solution)/shard_map/ppermute | solution.py:17
  37.3 5.9 %collective-permute-done.4 = f32[2,1,128,256]{3,0,2,1:T(2,128)S(1)} collective-permute-done((f32[2,1,128,256]{3,0,2,1:T(2,128)S(1)}, f32[2,1,128,256]{3,0,2,1:T(2,128)S(1)}, u32[]{:S(2)}, u32[]{:S(2)}) %collective-permute-start.4) | collective-permute-done | bytes 262176 | tf_op jit(solution)/shard_map/ppermute | solution.py:20
  45.2 2.5 %fusion.22 = (bf16[2,128,256]{2,1,0:T(8,128)(2,1)S(1)}, f32[2,2,128,256]{3,0,2,1:T(2,128)S(1)}) fusion(f32[2,2,128,1]{3,0,2,1:T(2,128)S(1)} %get-tuple-element.183, f32[2,2,128,255]{3,0,2,1:T(2,128)S(1)} %get-tuple-element.185, f32[2,2,128,255]{3,0,2,1:T(2,128)S(1)} %get-tuple-element.184, f32[2,2,128,1]{3,0,2,1:T(2,128)S(1)} %get-tuple-element.182, ...), kind=kLoop, calls=%fused_computation.44 | loop fusion | flops 2293760 | bytes 4849664 | tf_op jit(solution)/shard_map/reduce_sum | solution.py:72
  47.7 7.4 %all-gather = bf16[8,128,256]{2,1,0:T(8,128)(2,1)S(1)} all-gather(bf16[2,128,256]{2,1,0:T(8,128)(2,1)S(1)} %get-tuple-element.176), channel_id=2, replica_groups=mesh['space'=8,'member'=4] {'member'}, dimensions={0}, use_global_device_ids=true | all-gather | bytes 655360 | tf_op jit(solution)/shard_map/all_gather | solution.py:74
  55.5 0.9 convolution_bitcast_fusion
  56.7 21.1 %while.19 = (s32[]{:T(128)}, f32[2,8]{1,0:T(2,128)S(1)}, bf16[2,65536]{1,0:T(2,128)(2,1)S(1)}, bf16[2,65536]{1,0:T(2,128)(2,1)S(1)}, s32[]{:T(128)}, /*index=5*/...) while((s32[]{:T(128)}, f32[2,8]{1,0:T(2,128)S(1)}, ...), condition=%wide.region_3.4_spmd, body=%wide.region_2.3_spmd.sunk | while | flops 524306 | bytes 2097520 | solution.py:104
  57.2 5.4 %collective-permute-done = bf16[2,65536]{1,0:T(2,128)(2,1)S(1)} collective-permute-done((bf16[2,65536]{1,0:T(2,128)(2,1)S(1)}, bf16[2,65536]{1,0:T(2,128)(2,1)S(1)}, u32[]{:S(2)}, u32[]{:S(2)}) %collective-permute-start) | collective-permute-done | bytes 262176 | tf_op jit(solution)/shard_map/while/body/eval_jaxpr/ppermute | solution.py:28
  63.9 5.8 %collective-permute-done = bf16[2,65536]{1,0:T(2,128)(2,1)S(1)} collective-permute-done((bf16[2,65536]{1,0:T(2,128)(2,1)S(1)}, bf16[2,65536]{1,0:T(2,128)(2,1)S(1)}, u32[]{:S(2)}, u32[]{:S(2)}) %collective-permute-start) | collective-permute-done | bytes 262176 | tf_op jit(solution)/shard_map/while/body/eval_jaxpr/ppermute | solution.py:28
  69.6 0.8 fusion.44
  70.9 5.8 %collective-permute-done = bf16[2,65536]{1,0:T(2,128)(2,1)S(1)} collective-permute-done((bf16[2,65536]{1,0:T(2,128)(2,1)S(1)}, bf16[2,65536]{1,0:T(2,128)(2,1)S(1)}, u32[]{:S(2)}, u32[]{:S(2)}) %collective-permute-start) | collective-permute-done | bytes 262176 | tf_op jit(solution)/shard_map/while/body/eval_jaxpr/ppermute | solution.py:28
  76.7 0.8 fusion.44
  77.9 0.8 copy.32
  78.7 23.3 %psum.7 = f32[2,8]{1,0:T(2,128)S(1)} all-reduce(f32[2,8]{1,0:T(2,128)S(1)} %broadcast_multiply_fusion), channel_id=1, replica_groups=mesh['space'=8,'member'=4] {'space'}, use_global_device_ids=true, to_apply=%region_4.5 | all-reduce | flops 16 | bytes 128 | tf_op jit(solution)/shard_map/psum | solution.py:106
  102.0 5.1 %all-gather.1 = f32[4,2,8]{2,1,0:T(2,128)S(1)} all-gather(f32[1,2,8]{2,1,0:T(2,128)S(1)} %bitcast.57), channel_id=1, replica_groups=mesh['space'=8,'member'=4] {'member'}, dimensions={0}, use_global_device_ids=true | all-gather | bytes 320 | tf_op jit(solution)/shard_map/all_gather | solution.py:107
  108.7 1.2 %select_bitcast_fusion = f32[8,8]{1,0:T(8,128)} fusion(f32[8,8]{0,1:T(8,128)S(1)} %copy.30, pred[]{:T(512)} %compare_reduce_fusion), kind=kLoop, calls=%fused_computation.33 | loop fusion | flops 192 | bytes 513 | tf_op jit(solution)/shard_map/transpose | solution.py:110
  (43 shorter events, 9.1 us)
Async XLA Ops:
  0.6 18.2 %copy-start.1 = (s32[2]{0:T(128)S(1)}, s32[2]{0:T(128)}, u32[]{:S(2)}) copy-start(s32[2]{0:T(128)} %param.15) | copy-start | bytes 28
  2.3 16.0 %collective-permute-start.1 = (f32[2,1,128,256]{3,0,2,1:T(2,128)S(1)}, f32[2,1,128,256]{3,0,2,1:T(2,128)S(1)}, u32[]{:S(2)}, u32[]{:S(2)}) collective-permute-start(f32[2,1,128,256]{3,0,2,1:T(2,128)S(1)} %get-tuple-element.196), channel_id=1, source_target_pairs={{0,4},{4,8},{8,12},{12,16},{16,20},{20,24},{24,28},{1,5},{5,9},{9,... | collective-permute-start | bytes 786440 | tf_op jit(solution)/shard_map/ppermute | solution.py:17
  7.2 11.2 %collective-permute-start.2 = (f32[2,1,128,256]{3,0,2,1:T(2,128)S(1)}, f32[2,1,128,256]{3,0,2,1:T(2,128)S(1)}, u32[]{:S(2)}, u32[]{:S(2)}) collective-permute-start(f32[2,1,128,256]{3,0,2,1:T(2,128)S(1)} %get-tuple-element.197), channel_id=1, source_target_pairs={{4,0},{8,4},{12,8},{16,12},{20,16},{24,20},{28,24},{5,1},{9,5},{13... | collective-permute-start | bytes 786440 | tf_op jit(solution)/shard_map/ppermute | solution.py:20
  18.8 7.3 %copy-start = (f32[2,128,256]{2,1,0:T(8,128)S(1)}, f32[2,128,256]{2,1,0:T(8,128)}, u32[]{:S(2)}) copy-start(f32[2,128,256]{2,1,0:T(8,128)} %param.12) | copy-start | bytes 786436
  28.3 9.1 %collective-permute-start.3 = (f32[2,1,128,256]{3,0,2,1:T(2,128)S(1)}, f32[2,1,128,256]{3,0,2,1:T(2,128)S(1)}, u32[]{:S(2)}, u32[]{:S(2)}) collective-permute-start(f32[2,1,128,256]{3,0,2,1:T(2,128)S(1)} %get-tuple-element.194), channel_id=1, source_target_pairs={{0,4},{4,8},{8,12},{12,16},{16,20},{20,24},{24,28},{1,5},{5,9},{9,... | collective-permute-start | bytes 786440 | tf_op jit(solution)/shard_map/ppermute | solution.py:17
  32.7 10.5 %collective-permute-start.4 = (f32[2,1,128,256]{3,0,2,1:T(2,128)S(1)}, f32[2,1,128,256]{3,0,2,1:T(2,128)S(1)}, u32[]{:S(2)}, u32[]{:S(2)}) collective-permute-start(f32[2,1,128,256]{3,0,2,1:T(2,128)S(1)} %get-tuple-element.195), channel_id=1, source_target_pairs={{4,0},{8,4},{12,8},{16,12},{20,16},{24,20},{28,24},{5,1},{9,5},{13... | collective-permute-start | bytes 786440 | tf_op jit(solution)/shard_map/ppermute | solution.py:20
  56.8 5.8 %collective-permute-start = (bf16[2,65536]{1,0:T(2,128)(2,1)S(1)}, bf16[2,65536]{1,0:T(2,128)(2,1)S(1)}, u32[]{:S(2)}, u32[]{:S(2)}) collective-permute-start(bf16[2,65536]{1,0:T(2,128)(2,1)S(1)} %get-tuple-element.244), channel_id=1, source_target_pairs={{3,0},{0,1},{1,2},{2,3},{7,4},{4,5},{5,6},{6,7},{11,8},{8,9},{9,10... | collective-permute-start | bytes 786440 | tf_op jit(solution)/shard_map/while/body/eval_jaxpr/ppermute | solution.py:28
  63.8 5.8 %collective-permute-start = (bf16[2,65536]{1,0:T(2,128)(2,1)S(1)}, bf16[2,65536]{1,0:T(2,128)(2,1)S(1)}, u32[]{:S(2)}, u32[]{:S(2)}) collective-permute-start(bf16[2,65536]{1,0:T(2,128)(2,1)S(1)} %get-tuple-element.244), channel_id=1, source_target_pairs={{3,0},{0,1},{1,2},{2,3},{7,4},{4,5},{5,6},{6,7},{11,8},{8,9},{9,10... | collective-permute-start | bytes 786440 | tf_op jit(solution)/shard_map/while/body/eval_jaxpr/ppermute | solution.py:28
  70.8 5.8 %collective-permute-start = (bf16[2,65536]{1,0:T(2,128)(2,1)S(1)}, bf16[2,65536]{1,0:T(2,128)(2,1)S(1)}, u32[]{:S(2)}, u32[]{:S(2)}) collective-permute-start(bf16[2,65536]{1,0:T(2,128)(2,1)S(1)} %get-tuple-element.244), channel_id=1, source_target_pairs={{3,0},{0,1},{1,2},{2,3},{7,4},{4,5},{5,6},{6,7},{11,8},{8,9},{9,10... | collective-permute-start | bytes 786440 | tf_op jit(solution)/shard_map/while/body/eval_jaxpr/ppermute | solution.py:28
